TPU v7x, 32 devices: a whole 2x2x4 slice. The times are simulated.
32 devices in a mesh: dp: 8 (over y, x, core), mp: 4 (over z).
Axes of the slice: x: 2, y: 2, z: 4, core: 2. Of those that a mesh axis runs over, the one named last changes fastest.
Arguments:
- tokens: bfloat16 [2048, 32768], P('dp', 'mp'), may hold values from -6 to 6
- block_weights: bfloat16 [128, 8, 256, 256], P('mp'), may hold values from -0.125 to 0.125
- lowrank_down: bfloat16 [32768, 256], P(('mp', 'dp')), may hold values from -0.03125 to 0.03125
- lowrank_up: bfloat16 [32768, 256], P(('mp', 'dp')), may hold values from -0.375 to 0.375
- cotangent: bfloat16 [2048, 32768], P('dp', 'mp'), may hold values from -6 to 6
- seq_lengths: int32 [8], P('dp'), may hold values from 64 to 256, as said below
Outputs:
- output: bfloat16 [2048, 32768], P('dp', 'mp')
- grad_tokens: bfloat16 [2048, 32768], P('dp', 'mp')
- grad_blocks: bfloat16 [128, 8, 256, 256], P(('mp', 'dp'))
- grad_lowrank: bfloat16 [32768, 2, 256], P(('mp', 'dp'))
Inputs may be any that keep to these rules, and one draw needn't show every extreme that they name: `seq_lengths`: each data shard holds one sequence in 256 slots, live from the first slot; some shard is full and some shard holds exactly 64 live tokens.
All inputs are finite; a program needn't handle non-finite values.
Results may differ from a plain program's by a relative error of at most 0.025.
Values may be sent and summed in bfloat16 or wider, within the bound.
A program may use at most 256 MiB of HBM per device.

v0:
```python
import jax
import jax.numpy as jnp
from jax import lax
from jax.sharding import PartitionSpec as P


def partner(value, axis, bit):
    mask = 2**bit
    pairs = [(source, source ^ mask) for source in range(lax.axis_size(axis))]
    return lax.ppermute(value, axis, pairs)


def activate(values):
    return jax.nn.gelu(values, approximate=True)


def flip_blocks(blk_array, depth, local_blocks):
    tok_rows = blk_array.shape[0]
    blk_size = blk_array.shape[2]
    stride_len = 2**depth
    if stride_len < local_blocks:
        grouped = blk_array.reshape(
            tok_rows, local_blocks // (2 * stride_len), 2, stride_len, blk_size
        )
        return jnp.flip(grouped, 2).reshape(tok_rows, local_blocks, blk_size)
    swap_bit = (stride_len // local_blocks).bit_length() - 1
    return partner(blk_array, "mp", swap_bit)


def per_device(tokens, block_weights, lowrank_down, lowrank_up, cotangent, seq_lengths):
    tok_rows = tokens.shape[0]
    features = tokens.shape[1]
    local_blocks = block_weights.shape[0]
    level_count = block_weights.shape[1]
    blk_size = block_weights.shape[2]
    down_factor, up_factor = (
        lax.all_gather(lowrank_down, "dp", axis=0, tiled=True),
        lax.all_gather(lowrank_up, "dp", axis=0, tiled=True),
    )
    live = (jnp.arange(tok_rows, dtype=jnp.int32) < seq_lengths[0]).astype(jnp.float32)[:, None]
    tok_blocks = tokens.reshape(tok_rows, local_blocks, blk_size)
    partners = [tok_blocks] + [
        flip_blocks(tok_blocks, depth, local_blocks) for depth in range(level_count - 1)
    ]
    stacked = jnp.stack(partners, 2)
    down_sum = lax.psum(
        jnp.dot(tokens, down_factor, preferred_element_type=jnp.float32).astype(jnp.bfloat16), "mp"
    )
    butterfly = jnp.einsum(
        "tblc,blcd->tbd", stacked, block_weights, preferred_element_type=jnp.float32
    )
    hidden = butterfly.reshape(tok_rows, features) + jnp.dot(
        down_sum, up_factor.T, preferred_element_type=jnp.float32
    )
    output = (live * activate(hidden)).astype(jnp.bfloat16)
    _, pullback = jax.vjp(activate, hidden)
    (pre_grad,) = pullback(live * cotangent.astype(jnp.float32))
    grad_hidden = pre_grad.astype(jnp.bfloat16)
    up_sum = lax.psum(
        jnp.dot(grad_hidden, up_factor, preferred_element_type=jnp.float32).astype(jnp.bfloat16),
        "mp",
    )
    hid_blocks = grad_hidden.reshape(tok_rows, local_blocks, blk_size)
    outgoing = jnp.einsum(
        "tbd,blcd->tblc", hid_blocks, block_weights, preferred_element_type=jnp.float32
    ).astype(jnp.bfloat16)
    accumulated = outgoing[:, :, 0].astype(jnp.float32)
    for depth in range(level_count - 1):
        accumulated = accumulated + flip_blocks(
            outgoing[:, :, depth + 1], depth, local_blocks
        ).astype(jnp.float32)
    grad_tokens = accumulated.reshape(tok_rows, features) + jnp.dot(
        up_sum, down_factor.T, preferred_element_type=jnp.float32
    )
    grad_tokens = grad_tokens.astype(jnp.bfloat16)
    grad_blocks = lax.psum_scatter(
        jnp.einsum(
            "tblc,tbd->blcd", stacked, hid_blocks, preferred_element_type=jnp.float32
        ).astype(jnp.bfloat16),
        "dp",
        scatter_dimension=0,
        tiled=True,
    )
    grad_down = jnp.einsum("tf,tr->fr", tokens, up_sum, preferred_element_type=jnp.float32)
    grad_up = jnp.einsum("tf,tr->fr", grad_hidden, down_sum, preferred_element_type=jnp.float32)
    grad_lowrank = lax.psum_scatter(
        jnp.stack([grad_down, grad_up], 1).astype(jnp.bfloat16),
        "dp",
        scatter_dimension=0,
        tiled=True,
    )
    return (output, grad_tokens, grad_blocks, grad_lowrank)


def solution(mesh):
    placed = (
        P("dp", "mp"),
        P("mp", None, None, None),
        P(("mp", "dp"), None),
        P(("mp", "dp"), None),
        P("dp", "mp"),
        P("dp"),
    )
    return jax.shard_map(
        per_device,
        mesh=mesh,
        in_specs=placed,
        out_specs=(
            P("dp", "mp"),
            P("dp", "mp"),
            P(("mp", "dp"), None, None, None),
            P(("mp", "dp"), None, None),
        ),
        check_vma=False,
    )
```

profile of v0, /device:TPU:0, one launch (start us, length us, event | category | flops | bytes accessed | tf_op | source)
XLA Modules:
  0.0 642.1 jit_solution(4565502180161951914)
XLA Ops:
  8.7 6.4 copy.26
  15.1 6.5 %copy.33 = bf16[256,32,256]{2,0,1:T(8,128)(2,1)} copy(bf16[256,32,256]{0,2,1:T(8,128)(2,1)} %bitcast.94) | data formatting | bytes 8388608 | tf_op jit(solution)/shard_map/reshape | solution.py:41
  27.3 7.9 %reshape_reshape.17 = bf16[256,4,2,4,256]{4,3,2,1,0:T(4,128)(2,1)} reshape(bf16[256,8192]{1,0:T(8,128)(2,1)} %param.6) | data formatting | bytes 8388608 | tf_op jit(solution)/shard_map/reshape;reshape | solution.py:22
  35.2 7.8 %reshape_reshape.16 = bf16[256,8,2,2,256]{4,3,2,1,0:T(2,128)(2,1)} reshape(bf16[256,8192]{1,0:T(8,128)(2,1)} %param.6) | data formatting | bytes 8388608 | tf_op jit(solution)/shard_map/reshape;reshape | solution.py:22
  43.0 7.8 %reshape_reshape.15 = bf16[256,16,2,1,256]{4,2,1,0,3:T(2,128)(2,1)} reshape(bf16[256,8192]{1,0:T(8,128)(2,1)} %param.6) | data formatting | bytes 8388608 | tf_op jit(solution)/shard_map/reshape;reshape | solution.py:22
  57.1 6.6 %copy.35 = bf16[256,32,1,256]{3,0,2,1:T(8,128)(2,1)} copy(bf16[256,32,1,256]{0,3,1,2:T(8,128)(2,1)} %bitcast.95) | data formatting | bytes 8388608 | tf_op jit(solution)/shard_map/stack;reshape | solution.py:45
  63.7 6.6 %copy.31 = bf16[256,1,2,16,256]{4,0,3,2,1:T(8,128)(2,1)} copy(bf16[256,1,2,16,256]{4,3,2,0,1:T(8,128)(2,1)} %bitcast.96) | data formatting | bytes 8388608 | tf_op jit(solution)/shard_map/reshape;reshape | solution.py:22
  74.8 6.6 %copy.30 = bf16[256,2,2,8,256]{4,0,3,2,1:T(8,128)(2,1)} copy(bf16[256,2,2,8,256]{4,3,2,1,0:T(8,128)(2,1)} %bitcast.97) | data formatting | bytes 8388608 | tf_op jit(solution)/shard_map/reshape;reshape | solution.py:22
  86.0 6.6 %copy.29 = bf16[256,4,2,4,256]{4,0,3,2,1:T(8,128)(2,1)} copy(bf16[256,4,2,4,256]{4,3,2,1,0:T(4,128)(2,1)} %reshape_reshape.17) | data formatting | bytes 8388608 | tf_op jit(solution)/shard_map/reshape;reshape | solution.py:22
  97.3 6.6 %copy.28 = bf16[256,8,2,2,256]{4,0,3,2,1:T(8,128)(2,1)} copy(bf16[256,8,2,2,256]{4,3,2,1,0:T(2,128)(2,1)} %reshape_reshape.16) | data formatting | bytes 8388608 | tf_op jit(solution)/shard_map/reshape;reshape | solution.py:22
  108.4 7.0 %copy.27 = bf16[256,16,2,1,256]{4,0,2,1,3:T(8,128)(2,1)} copy(bf16[256,16,2,1,256]{4,2,1,0,3:T(2,128)(2,1)} %reshape_reshape.15) | data formatting | bytes 8388608 | tf_op jit(solution)/shard_map/reshape;reshape | solution.py:22
  137.3 67.9 %collective-permute-done = bf16[256,32,256]{2,0,1:T(8,128)(2,1)} collective-permute-done((bf16[256,32,256]{2,0,1:T(8,128)(2,1)}, bf16[256,32,256]{2,0,1:T(8,128)(2,1)}, u32[]{:S(2)}, u32[]{:S(2)}) %collective-permute-start) | collective-permute-done | bytes 4194336 | tf_op jit(solution)/shard_map/ppermute | solution.py:10
  219.8 26.0 %fusion.14 = f32[32,256,256,1]{1,2,3,0:T(8,128)} fusion(bf16[256,32,8,256]{3,0,2,1:T(8,128)(2,1)} %bitcast_dynamic-update-slice_fusion, bf16[32,8,256,256]{3,2,1,0:T(8,128)(2,1)} %param.7), kind=kOutput, calls=%fused_computation.42 | convolution fusion | flops 8589934592 | bytes 75497472 | tf_op jit(solution)/shard_map/tblc,blcd->tbd/dot_general | solution.py:49
  245.8 8.9 %copy.37 = f32[256,8192]{1,0:T(8,128)} copy(f32[256,8192]{0,1:T(8,128)} %bitcast.93) | data formatting | bytes 16777216 | tf_op jit(solution)/shard_map/reshape | solution.py:52
  259.4 9.9 %fusion.8 = (bf16[256,8192]{1,0:T(8,128)(2,1)S(1)}, bf16[256,8192]{1,0:T(8,128)(2,1)}) fusion(bf16[256,8192]{1,0:T(8,128)(2,1)} %param.10, f32[256]{0:T(256)S(1)} %compare_convert_fusion, f32[256,8192]{1,0:T(8,128)S(1)} %copy-done.2, f32[256,8192]{1,0:T(8,128)S(1)} %fusion.15), kind=kLoop, calls=%fused_computation.14 | loop fusion | flops 54525952 | bytes 29361152 | tf_op jit(solution)/shard_map/convert_element_type | solution.py:58
  281.0 29.4 %all-reduce.5.cloned.1.call-done = bf16[256,256]{1,0:T(8,128)(2,1)} async-done(((bf16[256,256]{1,0:T(8,128)(2,1)}), bf16[256,256]{1,0:T(8,128)(2,1)}) %all-reduce.5.cloned.1.call-update) | async-done | bytes 131088 | tf_op jit(solution)/shard_map/psum | solution.py:59
  328.0 43.8 %convolution_convert_fusion = bf16[32,8,256,256]{3,2,1,0:T(8,128)(2,1)} fusion(bf16[256,32,8,256]{3,0,2,1:T(8,128)(2,1)} %bitcast_dynamic-update-slice_fusion, bf16[256,32,256,1]{2,1,0,3:T(8,128)(2,1)S(1)} %bitcast.91), kind=kOutput, calls=%fused_computation.1 | convolution fusion | flops 8606711808 | bytes 71303168 | tf_op jit(solution)/shard_map/tblc,tbd->blcd/dot_general | solution.py:77
  371.8 24.8 %convert_bitcast_fusion = bf16[256,32,8,256]{0,3,2,1:T(8,128)(2,1)} fusion(bf16[32,8,256,256]{3,2,1,0:T(8,128)(2,1)} %param.7, bf16[256,32,256,1]{2,1,0,3:T(8,128)(2,1)} %bitcast.92), kind=kOutput, calls=%fused_computation | convolution fusion | flops 8606711808 | bytes 71303168 | tf_op jit(solution)/shard_map/tbd,blcd->tblc/dot_general | solution.py:64
  396.7 23.5 %fusion.13 = (bf16[256,32,1,256]{0,3,2,1:T(8,128)(2,1)}, bf16[256,32,256]{0,2,1:T(8,128)(2,1)}, bf16[256,32,1,256]{0,3,2,1:T(8,128)(2,1)}, bf16[256,32,1,256]{0,...) fusion(bf16[256,32,8,256]{0,3,2,1:T(8,128)(2,1)} %convert_bitca, ...), kind=kLoop, calls=%fused_computation.41 | loop fusion | bytes 58720256 | tf_op jit(solution)/shard_map/slice | solution.py:70
  450.7 8.0 %fusion.16 = f32[256,8192]{1,0:T(8,128)} fusion(bf16[256,256]{1,0:T(8,128)(2,1)S(1)} %copy-done.12, bf16[8192,256]{1,0:T(8,128)(2,1)} %all-gather.3.cloned.1.call-done), kind=kOutput, calls=%fused_computation.44 | convolution fusion | flops 1073741824 | bytes 12713984 | tf_op jit(solution)/shard_map/dot_general | solution.py:72
  458.6 142.9 %collective-permute-done.3 = bf16[256,32,256]{0,2,1:T(8,128)(2,1)} collective-permute-done((bf16[256,32,256]{0,2,1:T(8,128)(2,1)}, bf16[256,32,256]{0,2,1:T(8,128)(2,1)}, u32[]{:S(2)}, u32[]{:S(2)}) %collective-permute-start.3) | collective-permute-done | bytes 4194336 | tf_op jit(solution)/shard_map/ppermute | solution.py:10
  601.6 12.1 %fusion.10 = f32[256,32,256]{0,2,1:T(8,128)} fusion(bf16[256,32,256]{0,2,1:T(8,128)(2,1)} %collective-permute-done.3, bf16[256,32,256]{0,2,1:T(8,128)(2,1)} %collective-permute-done.2, bf16[256,32,8,256]{0,3,2,1:T(8,128)(2,1)} %convert_bitcast_fusion, bf16[256,1,2,16,256]{0,4,3,2,1:T(8,128)(2,1)S(1)} %copy-done.4, ...), kind=kLoop, calls=%fused_computation.18 | loop fusion | flops 31457280 | bytes 41943040 | tf_op jit(solution)/shard_map/add | solution.py:69
  613.7 8.9 %copy.41 = f32[256,8192]{1,0:T(8,128)} copy(f32[256,8192]{0,1:T(8,128)} %bitcast.98) | data formatting | bytes 16777216 | tf_op jit(solution)/shard_map/reshape | solution.py:72
  622.6 8.8 %add_convert_fusion = bf16[256,8192]{1,0:T(8,128)(2,1)} fusion(f32[256,8192]{1,0:T(8,128)} %copy.41, f32[256,8192]{1,0:T(8,128)} %fusion.16), kind=kLoop, calls=%fused_computation.23 | loop fusion | flops 4194304 | bytes 20971520 | tf_op jit(solution)/shard_map/convert_element_type | solution.py:75
  (79 shorter events, 135.8 us)
Async XLA Ops:
  7.2 207.2 %all-gather.3.cloned.1.call-start = ((), (), s32[]{:S(2)}) async-start(), calls=%async_computation.2 | async-start | bytes 4718592 | tf_op jit(solution)/shard_map/all_gather | solution.py:37
  7.9 246.8 %all-gather.5.cloned.1.call-start = ((), (), s32[]{:S(2)}) async-start(), calls=%async_computation.4 | async-start | bytes 4718592 | tf_op jit(solution)/shard_map/all_gather | solution.py:38
  8.6 246.0 %all-reduce.3.cloned.1.call-start = ((), (), s32[]{:S(2)}) async-start(), calls=%async_computation.3 | async-start | bytes 262144 | tf_op jit(solution)/shard_map/psum | solution.py:46
  21.6 183.6 %collective-permute-start = (bf16[256,32,256]{2,0,1:T(8,128)(2,1)}, bf16[256,32,256]{2,0,1:T(8,128)(2,1)}, u32[]{:S(2)}, u32[]{:S(2)}) collective-permute-start(bf16[256,32,256]{2,0,1:T(8,128)(2,1)} %copy.33), channel_id=1, source_target_pairs={{0,1},{1,0},{2,3},{3,2},{4,5},{5,4},{6,7},{7,6},{8,9},{9,8},{10,11... | collective-permute-start | bytes 12582920 | tf_op jit(solution)/shard_map/ppermute | solution.py:10
  24.7 185.1 %collective-permute-start.1 = (bf16[256,32,256]{2,0,1:T(8,128)(2,1)}, bf16[256,32,256]{2,0,1:T(8,128)(2,1)}, u32[]{:S(2)}, u32[]{:S(2)}) collective-permute-start(bf16[256,32,256]{2,0,1:T(8,128)(2,1)} %copy.33), channel_id=1, source_target_pairs={{0,2},{1,3},{2,0},{3,1},{4,6},{5,7},{6,4},{7,5},{8,10},{9,11},{10,... | collective-permute-start | bytes 12582920 | tf_op jit(solution)/shard_map/ppermute | solution.py:10
  120.0 4.9 copy-start.10
  120.0 7.3 %copy-start.9 = (bf16[256,8,2,2,256]{4,0,3,2,1:T(8,128)(2,1)S(1)}, bf16[256,8,2,2,256]{4,0,3,2,1:T(8,128)(2,1)}, u32[]{:S(2)}) copy-start(bf16[256,8,2,2,256]{4,0,3,2,1:T(8,128)(2,1)} %rev.36) | copy-start | bytes 12582916
  124.9 5.0 copy-start.8
  127.4 5.6 copy-start.7
  129.9 5.2 copy-start.6
  219.8 90.6 %all-reduce.5.cloned.1.call-start = ((), (), s32[]{:S(2)}) async-start(), calls=%async_computation.5 | async-start | bytes 262144 | tf_op jit(solution)/shard_map/psum | solution.py:59
  254.7 4.7 copy-start.2
  269.2 2.0 copy-start
  269.2 6.2 copy-start.13
  275.4 356.0 %reduce-scatter.5.cloned.1.call-start = ((), (), s32[]{:S(2)}) async-start(), calls=%async_computation.7 | async-start | bytes 9437184 | tf_op jit(solution)/shard_map/reduce_scatter | solution.py:86
  310.4 5.7 copy-start.11
  322.3 312.7 %reduce-scatter.3.cloned.1.call-start = ((), (), s32[]{:S(2)}) async-start(), calls=%async_computation.6 | async-start | bytes 37748736 | tf_op jit(solution)/shard_map/reduce_scatter | solution.py:76
  325.9 2.1 copy-start.1
  420.2 181.4 %collective-permute-start.3 = (bf16[256,32,256]{0,2,1:T(8,128)(2,1)}, bf16[256,32,256]{0,2,1:T(8,128)(2,1)}, u32[]{:S(2)}, u32[]{:S(2)}) collective-permute-start(bf16[256,32,256]{0,2,1:T(8,128)(2,1)} %get-tuple-element.13), channel_id=1, source_target_pairs={{0,2},{1,3},{2,0},{3,1},{4,6},{5,7},{6,4},{7,5},{8,10},{9,11},{10,... | collective-permute-start | bytes 12582920 | tf_op jit(solution)/shard_map/ppermute | solution.py:10
  422.0 179.6 %collective-permute-start.2 = (bf16[256,32,256]{0,2,1:T(8,128)(2,1)}, bf16[256,32,256]{0,2,1:T(8,128)(2,1)}, u32[]{:S(2)}, u32[]{:S(2)}) collective-permute-start(bf16[256,32,256]{0,2,1:T(8,128)(2,1)} %get-tuple-element.18), channel_id=1, source_target_pairs={{0,1},{1,0},{2,3},{3,2},{4,5},{5,4},{6,7},{7,6},{8,9},{9,8},{10,11... | collective-permute-start | bytes 12582920 | tf_op jit(solution)/shard_map/ppermute | solution.py:10
  440.3 10.3 %copy-start.12 = (bf16[256,256]{1,0:T(8,128)(2,1)S(1)}, bf16[256,256]{1,0:T(8,128)(2,1)}, u32[]{:S(2)}) copy-start(bf16[256,256]{1,0:T(8,128)(2,1)} %all-reduce.5.cloned.1.call-done) | copy-start | bytes 393220
  450.6 150.9 %copy-start.3 = (bf16[256,16,2,1,256]{0,4,2,1,3:T(8,128)(2,1)S(1)}, bf16[256,16,2,1,256]{0,4,2,1,3:T(8,128)(2,1)}, u32[]{:S(2)}) copy-start(bf16[256,16,2,1,256]{0,4,2,1,3:T(8,128)(2,1)} %rev.40) | copy-start | bytes 12582916
  450.6 150.9 %copy-start.4 = (bf16[256,1,2,16,256]{0,4,3,2,1:T(8,128)(2,1)S(1)}, bf16[256,1,2,16,256]{0,4,3,2,1:T(8,128)(2,1)}, u32[]{:S(2)}) copy-start(bf16[256,1,2,16,256]{0,4,3,2,1:T(8,128)(2,1)} %rev.44) | copy-start | bytes 12582916
  450.6 151.0 %copy-start.5 = (bf16[256,2,2,8,256]{0,4,3,2,1:T(8,128)(2,1)S(1)}, bf16[256,2,2,8,256]{0,4,3,2,1:T(8,128)(2,1)}, u32[]{:S(2)}) copy-start(bf16[256,2,2,8,256]{0,4,3,2,1:T(8,128)(2,1)} %rev.43) | copy-start | bytes 12582916
Sparse Core Ops, SparseCore 0:
  9.9 39.4 all-gather.2
  51.2 36.7 all-gather.4
  219.9 34.7 all-reduce.2
  275.5 34.8 all-reduce.4
  322.4 70.9 reduce-scatter.4
  397.8 205.2 reduce-scatter.2
where the time goes:
time: 648 us; the launch traced here: 642 us
  waiting for transfers between devices  242 us (37%)
  local copies, waits for them, and re-layouts  212 us (33%)
  matrix products  127 us (20%)
  other arithmetic  37 us (6%)
  between operations  15.1 us (2%)
  starting transfers between devices  9.09 us (1%)
    ppermute x4, waiting for transfers between devices, partner(): return lax.ppermute(value, axis, pairs)  211 us
    another operation x8, local copies, waits for them, and re-layouts, flip_blocks(): blk_array.reshape(tok_rows, local_blocks // (2 * stride_len), 2, stride_l...  56.8 us
    rev x10, local copies, waits for them, and re-layouts, flip_blocks(): return jnp.flip(grouped, 2).reshape(tok_rows, local_blocks, blk_size)  50.3 us
    unnamed x39, local copies, waits for them, and re-layouts  46.1 us
    dot_general x1, matrix products, per_device(): jnp.einsum('tblc,tbd->blcd', stacked, hid_blocks, preferred_element_type=...  43.8 us
    psum x1, waiting for transfers between devices, per_device(): lax.psum(jnp.dot(grad_hidden, up_factor, preferred_element_type=jnp.float...  29.4 us
    dot_general x1, matrix products, per_device(): jnp.einsum('tblc,blcd->tbd', stacked, block_weights, preferred_element_ty...  26 us
    dot_general x1, matrix products, per_device(): jnp.einsum('tbd,blcd->tblc', hid_blocks, block_weights, preferred_element...  24.8 us
  transfers between devices with their start and end apart: 10, of which 3 were waited for; matrix products, arithmetic and copies ran while one was open for 53% of the time, Pallas kernels for 0%

commit v1 on v0

v1 whole, which is shorter than its diff:
```python
import functools
import math

import jax
import jax.numpy as jnp
from jax import lax
from jax.experimental import pallas as pl
from jax.experimental.pallas import tpu as pltpu
from jax.sharding import PartitionSpec as P

F32 = jnp.float32
BF16 = jnp.bfloat16
VMEM_LIMIT = 48 * 2**20


def partner(value, axis, mask):
    pairs = [(source, source ^ mask) for source in range(lax.axis_size(axis))]
    return lax.ppermute(value, axis, pairs)


def dot(lhs, rhs, left, right):
    return lax.dot_general(lhs, rhs, (((left,), (right,)), ((), ())), preferred_element_type=F32)


def mp_sum(part):
    total = part.astype(F32)
    for mask in range(1, lax.axis_size("mp")):
        total = total + partner(part, "mp", mask).astype(F32)
    return total.astype(BF16)


def forward_kernel(n_local, n_remote, has_prev, seq_ref, *refs):
    levels = n_local + n_remote
    sources = refs[:levels]
    w_ref, up_ref, down_ref, cot_ref = refs[levels : levels + 4]
    outs = refs[levels + 4 + (2 if has_prev else 0) :]
    out_ref, g_ref, wgrad_ref, upsum_ref = outs[:4]
    term_refs = outs[4:]
    hidden = dot(down_ref[...], up_ref[...], 1, 1)
    for level in range(levels):
        hidden = hidden + dot(sources[level][...], w_ref[0, level], 1, 0)
    rows = lax.broadcasted_iota(jnp.int32, hidden.shape, 0)
    live = rows < seq_ref[0]
    root = math.sqrt(2.0 / math.pi)
    square = hidden * hidden
    slope = jnp.tanh(root * hidden * (1.0 + 0.044715 * square))
    cdf = 0.5 + 0.5 * slope
    out_ref[...] = jnp.where(live, hidden * cdf, 0.0).astype(BF16)
    deriv = cdf + (0.5 * root) * hidden * (1.0 - slope * slope) * (1.0 + (3 * 0.044715) * square)
    grad = jnp.where(live, cot_ref[...].astype(F32) * deriv, 0.0).astype(BF16)
    g_ref[...] = grad
    for index, term_ref in enumerate(term_refs):
        term_ref[...] = dot(grad, w_ref[0, n_local + index], 1, 1).astype(BF16)
    for level in range(levels):
        wgrad_ref[0, level] = dot(sources[level][...], grad, 0, 0).astype(BF16)

    @pl.when((pl.program_id(0) == 0) & (pl.program_id(1) == 0))
    def _():
        upsum_ref[...] = jnp.zeros_like(upsum_ref)

    upsum_ref[...] += dot(grad, up_ref[...], 1, 0)


def forward_chunk(
    chunk, sizes, seq, tokens, remote, weights, up_factor, down_sum, cotangent, prev, extra
):
    dp, quota, per, n_local, blk = sizes
    rows, features = tokens.shape
    rank = down_sum.shape[1]
    levels = weights.shape[1]

    def block(d, s):
        return d * quota + chunk * per + s

    def local_spec(mask):
        return pl.BlockSpec((rows, blk), lambda d, s: (0, block(d, s) ^ mask))

    masks = [0] + [2**bit for bit in range(n_local - 1)]
    packed_spec = pl.BlockSpec((rows, blk), lambda d, s: (0, d * per + s))
    any_spec = pl.BlockSpec(memory_space=pl.ANY)
    in_specs = (
        [pl.BlockSpec(memory_space=pltpu.SMEM)]
        + [local_spec(mask) for mask in masks]
        + [packed_spec for _ in remote]
        + [
            pl.BlockSpec((1, levels, blk, blk), lambda d, s: (block(d, s), 0, 0, 0)),
            pl.BlockSpec((blk, rank), lambda d, s: (block(d, s), 0)),
            pl.BlockSpec((rows, rank), lambda d, s: (0, 0)),
            local_spec(0),
        ]
        + [any_spec for _ in prev]
    )
    args = [seq] + [tokens for _ in masks] + list(remote)
    args += [weights, up_factor, down_sum, cotangent] + list(prev)
    aliases = {len(args) - 2: 0, len(args) - 1: 1} if prev else {}
    wide = jax.ShapeDtypeStruct((rows, features), BF16)
    packed = jax.ShapeDtypeStruct((rows, dp * per * blk), BF16)
    steps = dp * per
    return pl.pallas_call(
        functools.partial(forward_kernel, n_local, len(remote), bool(prev)),
        grid=(dp, per),
        in_specs=in_specs,
        out_specs=[
            local_spec(0),
            local_spec(0),
            pl.BlockSpec((1, levels, blk, blk), lambda d, s: (d, s, 0, 0)),
            pl.BlockSpec((rows, rank), lambda d, s: (0, 0)),
        ]
        + [packed_spec for _ in remote],
        out_shape=[
            wide,
            wide,
            jax.ShapeDtypeStruct((dp, per * levels + extra, blk, blk), BF16),
            jax.ShapeDtypeStruct((rows, rank), F32),
        ]
        + [packed for _ in remote],
        input_output_aliases=aliases,
        compiler_params=pltpu.CompilerParams(vmem_limit_bytes=VMEM_LIMIT),
        cost_estimate=pl.CostEstimate(
            flops=steps * 22 * 2 * rows * blk * blk,
            bytes_accessed=steps * 4 * 2**20,
            transcendentals=steps * rows * blk,
        ),
        name="forward_%d" % chunk,
    )(*args)


def factor_kernel(tok_ref, g_ref, up_ref, down_ref, buf_ref, out_ref):
    out_ref[0, 0] = dot(tok_ref[...], up_ref[...], 0, 0).astype(BF16)
    out_ref[0, 1] = dot(g_ref[...], down_ref[...], 0, 0).astype(BF16)


def factor_grads(sizes, tokens, grad_hidden, up_sum, down_sum, buffer, offset):
    dp, quota, per, n_local, blk = sizes
    rows = tokens.shape[0]
    rank = up_sum.shape[1]
    col = pl.BlockSpec((rows, blk), lambda d, s: (0, d * quota + s))
    whole = pl.BlockSpec((rows, rank), lambda d, s: (0, 0))
    return pl.pallas_call(
        factor_kernel,
        grid=(dp, quota),
        in_specs=[col, col, whole, whole, pl.BlockSpec(memory_space=pl.ANY)],
        out_specs=pl.BlockSpec((1, 2, blk, rank), lambda d, s: (d, offset // 2 + s, 0, 0)),
        out_shape=jax.ShapeDtypeStruct(buffer.shape, BF16),
        input_output_aliases={4: 0},
        compiler_params=pltpu.CompilerParams(vmem_limit_bytes=VMEM_LIMIT),
        cost_estimate=pl.CostEstimate(
            flops=dp * quota * 4 * rows * blk * rank,
            bytes_accessed=dp * quota * 2**19,
            transcendentals=0,
        ),
        name="factor_grads",
    )(tokens, grad_hidden, up_sum, down_sum, buffer)


def backward_kernel(n_local, *refs):
    g_refs, w_refs = refs[:n_local], refs[n_local : 2 * n_local]
    up_ref, down_ref, out_ref = refs[2 * n_local :]
    total = dot(up_ref[...], down_ref[...], 1, 1)
    for level in range(n_local):
        total = total + dot(g_refs[level][...], w_refs[level][0, 0], 1, 1)
    out_ref[...] = total


def backward_local(sizes, grad_hidden, weights, up_sum, down_factor):
    dp, quota, per, n_local, blk = sizes
    rows, features = grad_hidden.shape
    rank = up_sum.shape[1]
    blocks = weights.shape[0]

    def g_spec(mask):
        return pl.BlockSpec((rows, blk), lambda j: (0, j ^ mask))

    def w_spec(mask, level):
        return pl.BlockSpec((1, 1, blk, blk), lambda j: (j ^ mask, level, 0, 0))

    masks = [0] + [2**bit for bit in range(n_local - 1)]
    return pl.pallas_call(
        functools.partial(backward_kernel, n_local),
        grid=(blocks,),
        in_specs=[g_spec(mask) for mask in masks]
        + [w_spec(mask, level) for level, mask in enumerate(masks)]
        + [
            pl.BlockSpec((rows, rank), lambda j: (0, 0)),
            pl.BlockSpec((blk, rank), lambda j: (j, 0)),
        ],
        out_specs=g_spec(0),
        out_shape=jax.ShapeDtypeStruct((rows, features), F32),
        compiler_params=pltpu.CompilerParams(vmem_limit_bytes=VMEM_LIMIT),
        cost_estimate=pl.CostEstimate(
            flops=blocks * (n_local + 1) * 2 * rows * blk * blk,
            bytes_accessed=blocks * 2 * 2**20,
            transcendentals=0,
        ),
        name="backward_local",
    )(*([grad_hidden] * n_local), *([weights] * n_local), up_sum, down_factor)


def finish_kernel(n_remote, *refs):
    total = refs[0][...]
    for term_ref in refs[1 : 1 + n_remote]:
        total = total + term_ref[...].astype(F32)
    refs[-1][...] = total.astype(BF16)


def finish_chunk(chunk, sizes, partial, landed, prev):
    dp, quota, per, n_local, blk = sizes
    rows, features = partial.shape
    width = per * blk
    chunks = quota // per
    spec = pl.BlockSpec((rows, width), lambda d: (0, d * chunks + chunk))
    packed_spec = pl.BlockSpec((rows, width), lambda d: (0, d))
    return pl.pallas_call(
        functools.partial(finish_kernel, len(landed)),
        grid=(dp,),
        in_specs=[spec]
        + [packed_spec for _ in landed]
        + [pl.BlockSpec(memory_space=pl.ANY) for _ in prev],
        out_specs=spec,
        out_shape=jax.ShapeDtypeStruct((rows, features), BF16),
        input_output_aliases={1 + len(landed): 0} if prev else {},
        compiler_params=pltpu.CompilerParams(vmem_limit_bytes=VMEM_LIMIT),
        cost_estimate=pl.CostEstimate(
            flops=dp * rows * width * 3,
            bytes_accessed=dp * rows * width * 10,
            transcendentals=0,
        ),
        name="finish_%d" % chunk,
    )(partial, *landed, *prev)


def per_device(tokens, block_weights, lowrank_down, lowrank_up, cotangent, seq_lengths):
    rows = tokens.shape[0]
    local_blocks, levels, blk = block_weights.shape[:3]
    rank = lowrank_down.shape[1]
    dp = lax.axis_size("dp")
    quota = local_blocks // dp
    chunks = 2 if quota % 2 == 0 else 1
    per = quota // chunks
    n_local = local_blocks.bit_length()
    remote_masks = [2**bit for bit in range(levels - n_local)]
    sizes = (dp, quota, per, n_local, blk)
    width = per * blk

    down_factor = lax.all_gather(lowrank_down, "dp", axis=0, tiled=True)
    up_factor = lax.all_gather(lowrank_up, "dp", axis=0, tiled=True)

    arrived = []
    for chunk in range(chunks):
        starts = [(d * chunks + chunk) * width for d in range(dp)]
        sent = jnp.concatenate([tokens[:, at : at + width] for at in starts], axis=1)
        if chunk:
            sent, arrived[-1] = lax.optimization_barrier((sent, arrived[-1]))
        arrived.append([partner(sent, "mp", mask) for mask in remote_masks])

    down_part = jnp.dot(tokens, down_factor, preferred_element_type=F32).astype(BF16)
    down_sum = mp_sum(down_part)

    prev = ()
    pending, wgrads = [], []
    up_part = None
    for chunk in range(chunks):
        last = chunk == chunks - 1
        out, grad_hidden, wgrad, up_chunk, *terms = forward_chunk(
            chunk,
            sizes,
            seq_lengths,
            tokens,
            arrived[chunk],
            block_weights,
            up_factor,
            down_sum,
            cotangent,
            prev,
            2 * quota if last else 0,
        )
        prev = (out, grad_hidden)
        up_part = up_chunk if up_part is None else up_part + up_chunk
        pending.append(terms)
        wgrads.append(wgrad)
        if not last:
            pending[-1], arrived[chunk + 1] = lax.optimization_barrier((terms, arrived[chunk + 1]))

    scattered = [
        lax.psum_scatter(wgrad, "dp", scatter_dimension=0, tiled=True) for wgrad in wgrads[:-1]
    ]
    up_sum = mp_sum(up_part.astype(BF16))
    returned = [
        [partner(term, "mp", mask) for term, mask in zip(terms, remote_masks)] for terms in pending
    ]
    merged = factor_grads(
        sizes, tokens, grad_hidden, up_sum, down_sum, wgrads[-1], per * levels
    )
    merged, scattered = lax.optimization_barrier((merged, scattered))
    scattered.append(lax.psum_scatter(merged, "dp", scatter_dimension=0, tiled=True))
    partial = backward_local(sizes, grad_hidden, block_weights, up_sum, down_factor)
    grad_tokens = ()
    for chunk in range(chunks):
        grad_tokens = (finish_chunk(chunk, sizes, partial, returned[chunk], grad_tokens),)

    pieces = [part[0, : per * levels] for part in scattered]
    grad_blocks = jnp.concatenate(pieces, axis=0).reshape(quota, levels, blk, blk)
    factors = scattered[-1][0, per * levels :].reshape(quota, 2, blk, rank)
    grad_lowrank = jnp.transpose(factors, (0, 2, 1, 3)).reshape(quota * blk, 2, rank)
    return (out, grad_tokens[0], grad_blocks, grad_lowrank)


def solution(mesh):
    placed = (
        P("dp", "mp"),
        P("mp", None, None, None),
        P(("mp", "dp"), None),
        P(("mp", "dp"), None),
        P("dp", "mp"),
        P("dp"),
    )
    return jax.shard_map(
        per_device,
        mesh=mesh,
        in_specs=placed,
        out_specs=(
            P("dp", "mp"),
            P("dp", "mp"),
            P(("mp", "dp"), None, None, None),
            P(("mp", "dp"), None, None),
        ),
        check_vma=False,
    )
```

time: 648 us -> 533 us (0.82)
  local copies, waits for them, and re-layouts: 212 us -> 25.5 us
  Pallas kernels: 0 us -> 137 us
  matrix products: 127 us -> 4.71 us
  waiting for transfers between devices: 242 us -> 323 us
  other arithmetic: 37 us -> 2.55 us
  starting transfers between devices: 9.09 us -> 23.8 us
    pallas_call x0 -> x6, Pallas kernels: none -> 137 us  [the longest x2 67.6 us: forward_chunk(): pl.pallas_call(functools.partial(forward_kernel, n_local, len(remote), bo...]
    dot_general x9 -> x1, matrix products: 127 us -> 4.71 us  [per_device(): jnp.dot(tokens, down_factor, preferred_element_type=F32).astype(BF16)]
    ppermute x4 -> x14, waiting for transfers between devices: 211 us -> 298 us  [partner(): return lax.ppermute(value, axis, pairs)]
    another operation x10 -> x0, local copies, waits for them, and re-layouts: 68.1 us -> none  [the longest x8 56.8 us: flip_blocks(): blk_array.reshape(tok_rows, local_blocks // (2 * stride_len), 2, stride_l...]
    rev x10 -> x0, local copies, waits for them, and re-layouts: 50.3 us -> none  [flip_blocks(): return jnp.flip(grouped, 2).reshape(tok_rows, local_blocks, blk_size)]
    psum x2 -> x0, waiting for transfers between devices: 29.4 us -> none  [the longest x1 29.4 us: per_device(): lax.psum(jnp.dot(grad_hidden, up_factor, preferred_element_type=jnp.float...]
    unnamed x39 -> x31, local copies, waits for them, and re-layouts: 46.1 us -> 21.4 us
    reshape x3 -> x0, local copies, waits for them, and re-layouts: 24.3 us -> none  [the longest x1 8.89 us: per_device(): butterfly.reshape(tok_rows, features)]
  transfers between devices with their start and end apart: 10 -> 18, of which waited for: 3 -> 12; matrix products, arithmetic and copies ran while one was open for 53% -> 3% of each run, Pallas kernels for 0% -> 19%
where the time goes in v1:
time: 533 us; the launch traced here: 531 us
  waiting for transfers between devices  323 us (61%)
  Pallas kernels  137 us (26%)
  local copies, waits for them, and re-layouts  25.5 us (5%)
  starting transfers between devices  23.8 us (4%)
  between operations  14.5 us (3%)
    ppermute x14, waiting for transfers between devices, partner(): return lax.ppermute(value, axis, pairs)  298 us
    pallas_call x2, Pallas kernels, forward_chunk(): pl.pallas_call(functools.partial(forward_kernel, n_local, len(remote), bo...  67.6 us
    pallas_call x1, Pallas kernels, backward_local(): pl.pallas_call(functools.partial(backward_kernel, n_local), grid=(blocks,...  34.7 us
    ppermute x14, starting transfers between devices, partner(): return lax.ppermute(value, axis, pairs)  23.7 us
    all_gather x1, waiting for transfers between devices, per_device(): down_factor = lax.all_gather(lowrank_down, 'dp', axis=0, tiled=True)  23.5 us
    pallas_call x1, Pallas kernels, factor_grads(): pl.pallas_call(factor_kernel, grid=(dp, quota), in_specs=[col, col, whole...  22.1 us
    unnamed x31, local copies, waits for them, and re-layouts  21.4 us
    pallas_call x2, Pallas kernels, finish_chunk(): pl.pallas_call(functools.partial(finish_kernel, len(landed)), grid=(dp,),...  12.7 us
  transfers between devices with their start and end apart: 18, of which 12 were waited for; matrix products, arithmetic and copies ran while one was open for 3% of the time, Pallas kernels for 19%

profile of v1, /device:TPU:0, one launch (start us, length us, event | category | flops | bytes accessed | tf_op | source)
XLA Modules:
  0.0 531.3 jit_solution(1156211028999161841)
XLA Ops:
  20.2 4.0 collective-permute-start.1
  25.9 23.5 %all-gather.5.cloned.1.call-done.refs_13_ = bf16[8192,256]{1,0:T(8,128)(2,1)} async-done(((bf16[1024,256]{1,0:T(8,128)(2,1)}), bf16[8192,256]{1,0:T(8,128)(2,1)}) %all-gather.5.cloned.1.call-update) | async-done | bytes 4194320 | tf_op jit(solution)/shard_map/all_gather | solution.py:245
  49.3 4.7 convolution_convert_fusion
  54.1 3.4 collective-permute-start.4
  59.2 57.6 %collective-permute-done.1.refs_7_ = bf16[256,4096]{1,0:T(8,128)(2,1)S(1)} collective-permute-done((bf16[256,4096]{1,0:T(8,128)(2,1)}, bf16[256,4096]{1,0:T(8,128)(2,1)S(1)}, u32[]{:S(2)}, u32[]{:S(2)}) %collective-permute-start.1) | collective-permute-done | bytes 2097184 | tf_op jit(solution)/shard_map/ppermute | solution.py:18
  116.8 2.2 collective-permute-done.refs_6_
  120.2 6.2 %collective-permute-done.3 = bf16[256,256]{1,0:T(8,128)(2,1)S(1)} collective-permute-done((bf16[256,256]{1,0:T(8,128)(2,1)S(1)}, bf16[256,256]{1,0:T(8,128)(2,1)S(1)}, u32[]{:S(2)}, u32[]{:S(2)}) %collective-permute-start.3) | collective-permute-done | bytes 131104 | tf_op jit(solution)/shard_map/ppermute | solution.py:18
  126.5 33.8 %forward_0.1 = (bf16[256,8192]{1,0:T(8,128)(2,1)}, bf16[256,8192]{1,0:T(8,128)(2,1)}, bf16[8,16,256,256]{3,2,1,0:T(8,128)(2,1)}, f32[256,256]{1,0:T(8,128)S(1)},...) custom-call(s32[1]{0:T(128)S(6)} %copy.33.seq_ref, bf16[256,8192]{1,0:T(8,128)(2,1)} %tok_ref.1, ...), custom_call_target="tpu_custom_call" | custom-call | flops 11811160064 | bytes 67108864 | tf_op jit(solution)/shard_map/forward_0/pallas_call | solution.py:99
  161.7 4.1 collective-permute-start.5
  165.8 88.9 %collective-permute-done.6.refs_7_ = bf16[256,4096]{1,0:T(8,128)(2,1)S(1)} collective-permute-done((bf16[256,4096]{1,0:T(8,128)(2,1)}, bf16[256,4096]{1,0:T(8,128)(2,1)S(1)}, u32[]{:S(2)}, u32[]{:S(2)}) %collective-permute-start.6) | collective-permute-done | bytes 2097184 | tf_op jit(solution)/shard_map/ppermute | solution.py:18
  256.7 33.8 %forward_1.1 = (bf16[256,8192]{1,0:T(8,128)(2,1)}, bf16[256,8192]{1,0:T(8,128)(2,1)}, bf16[8,24,256,256]{3,2,1,0:T(8,128)(2,1)}, f32[256,256]{1,0:T(8,128)S(1)},...) custom-call(s32[1]{0:T(128)S(6)} %copy.33.seq_ref, ...), custom_call_target="tpu_custom_call", output_to_operand_aliasing={{0}: (13, {}), {1}: (14, {})} | custom-call | flops 11811160064 | bytes 67108864 | tf_op jit(solution)/shard_map/forward_1/pallas_call | solution.py:99
  293.3 2.7 collective-permute-start.9
  297.8 3.3 collective-permute-done.9
  301.1 5.3 %collective-permute-done.8 = bf16[256,256]{1,0:T(8,128)(2,1)S(1)} collective-permute-done((bf16[256,256]{1,0:T(8,128)(2,1)S(1)}, bf16[256,256]{1,0:T(8,128)(2,1)S(1)}, u32[]{:S(2)}, u32[]{:S(2)}) %collective-permute-start.8) | collective-permute-done | bytes 131104 | tf_op jit(solution)/shard_map/ppermute | solution.py:18
  306.5 22.1 %factor_grads.1 = bf16[8,24,256,256]{3,2,1,0:T(8,128)(2,1)} custom-call(bf16[256,8192]{1,0:T(8,128)(2,1)S(1)} %copy-done.1, bf16[256,8192]{1,0:T(8,128)(2,1)} %get-tuple-element.35.refs_0_.refs_1_.refs_2_.refs_3_.refs_4_.refs_5_.g_ref, bf16[256,256]{1,0:T(8,128)(2,1)S(1)} %add_convert_fusion.refs_12_.up_ref, ...), custom_call_target="tpu_custom_call", output_to_operand_aliasing={{}: (4, {})} | custom-call | flops 2147483648 | bytes 16777216 | tf_op jit(solution)/shard_map/factor_grads/pallas_call | solution.py:139
  328.7 3.2 collective-permute-start.13
  333.6 3.2 copy-done.2
  336.8 34.7 %backward_local.1.refs_0_ = f32[256,8192]{1,0:T(8,128)} custom-call(bf16[256,8192]{1,0:T(8,128)(2,1)S(1)} %copy-done.2, bf16[256,8192]{1,0:T(8,128)(2,1)S(1)} %copy-done.2, bf16[256,8192]{1,0:T(8,128)(2,1)S(1)} %copy-done.2, bf16[256,8192]{1,0:T(8,128)(2,1)S(1)} %copy-done.2, bf16[256,8192]{1,0:T(8,128)(2,1)S(1)} %copy-done.2, ...), custom_call_target="tpu_custom_call" | custom-call | flops 7516192768 | bytes 67108864 | tf_op jit(solution)/shard_map/backward_local/pallas_call | solution.py:178
  371.5 91.7 %collective-permute-done.12.refs_1_ = bf16[256,4096]{1,0:T(8,128)(2,1)S(1)} collective-permute-done((bf16[256,4096]{1,0:T(8,128)(2,1)}, bf16[256,4096]{1,0:T(8,128)(2,1)S(1)}, u32[]{:S(2)}, u32[]{:S(2)}) %collective-permute-start.12) | collective-permute-done | bytes 2097184 | tf_op jit(solution)/shard_map/ppermute | solution.py:18
  463.2 6.4 %finish_0.1.refs_3_ = bf16[256,8192]{1,0:T(8,128)(2,1)} custom-call(f32[256,8192]{1,0:T(8,128)} %backward_local.1.refs_0_, bf16[256,4096]{1,0:T(8,128)(2,1)S(1)} %collective-permute-done.12.refs_1_, bf16[256,4096]{1,0:T(8,128)(2,1)S(1)} %collective-permute-done.13.refs_2_), custom_call_target="tpu_custom_call" | custom-call | flops 3145728 | bytes 10485760 | tf_op jit(solution)/shard_map/finish_0/pallas_call | solution.py:213
  469.6 40.1 %collective-permute-done.10.refs_1_ = bf16[256,4096]{1,0:T(8,128)(2,1)S(1)} collective-permute-done((bf16[256,4096]{1,0:T(8,128)(2,1)}, bf16[256,4096]{1,0:T(8,128)(2,1)S(1)}, u32[]{:S(2)}, u32[]{:S(2)}) %collective-permute-start.10) | collective-permute-done | bytes 2097184 | tf_op jit(solution)/shard_map/ppermute | solution.py:18
  511.2 6.3 %finish_1.1 = bf16[256,8192]{1,0:T(8,128)(2,1)} custom-call(f32[256,8192]{1,0:T(8,128)} %backward_local.1.refs_0_, bf16[256,4096]{1,0:T(8,128)(2,1)S(1)} %collective-permute-done.10.refs_1_, bf16[256,4096]{1,0:T(8,128)(2,1)S(1)} %collective-permute-done.11.refs_2_, bf16[256,8192]{1,0:T(8,128)(2,1)} %finish_0.1.refs_3_), custom_call_target="tpu_custom_call", output_to_operand_aliasing={{}: (3, {})} | custom-call | flops 3145728 | bytes 10485760 | tf_op jit(solution)/shard_map/finish_1/pallas_call | solution.py:213
  518.7 2.0 copy.14
  522.4 2.4 pad_maximum_fusion
  (63 shorter events, 31.1 us)
Async XLA Ops:
  7.2 42.2 %all-gather.5.cloned.1.call-start = ((), (), s32[]{:S(2)}) async-start(), calls=%async_computation.3 | async-start | bytes 4718592 | tf_op jit(solution)/shard_map/all_gather | solution.py:245
  7.9 118.6 %all-gather.3.cloned.1.call-start = ((), (), s32[]{:S(2)}) async-start(), calls=%async_computation.2 | async-start | bytes 4718592 | tf_op jit(solution)/shard_map/all_gather | solution.py:246
  8.6 320.0 %reduce-scatter.3.cloned.1.call-start = ((), (), s32[]{:S(2)}) async-start(), calls=%async_computation.4 | async-start | bytes 18874368 | tf_op jit(solution)/shard_map/reduce_scatter | solution.py:285
  8.7 7.2 %copy-start = (bf16[256,8192]{1,0:T(8,128)(2,1)S(1)}, bf16[256,8192]{1,0:T(8,128)(2,1)}, u32[]{:S(2)}) copy-start(bf16[256,8192]{1,0:T(8,128)(2,1)} %tok_ref.1) | copy-start | bytes 12582916
  20.2 96.6 %collective-permute-start.1 = (bf16[256,4096]{1,0:T(8,128)(2,1)}, bf16[256,4096]{1,0:T(8,128)(2,1)S(1)}, u32[]{:S(2)}, u32[]{:S(2)}) collective-permute-start(bf16[256,4096]{1,0:T(8,128)(2,1)} %get-tuple-element.46), channel_id=1, source_target_pairs={{0,2},{1,3},{2,0},{3,1},{4,6},{5,7},{6,4},{7,5},{8,10},{9,11},{10,... | collective-permute-start | bytes 6291464 | tf_op jit(solution)/shard_map/ppermute | solution.py:18
  24.3 94.8 %collective-permute-start = (bf16[256,4096]{1,0:T(8,128)(2,1)}, bf16[256,4096]{1,0:T(8,128)(2,1)}, u32[]{:S(2)}, u32[]{:S(2)}) collective-permute-start(bf16[256,4096]{1,0:T(8,128)(2,1)} %get-tuple-element.46), channel_id=1, source_target_pairs={{0,1},{1,0},{2,3},{3,2},{4,5},{5,4},{6,7},{7,6},{8,9},{9,8},{10,11... | collective-permute-start | bytes 6291464 | tf_op jit(solution)/shard_map/ppermute | solution.py:18
  54.1 66.1 %collective-permute-start.4 = (bf16[256,256]{1,0:T(8,128)(2,1)S(1)}, bf16[256,256]{1,0:T(8,128)(2,1)S(1)}, u32[]{:S(2)}, u32[]{:S(2)}) collective-permute-start(bf16[256,256]{1,0:T(8,128)(2,1)S(1)} %convolution_convert_fusion), channel_id=1, source_target_pairs={{0,3},{1,2},{2,1},{3,0},{4,7},{5,6},{6,5},{7,4},{8,11},{9,10},{10,... | collective-permute-start | bytes 393224 | tf_op jit(solution)/shard_map/ppermute | solution.py:18
  57.4 68.9 %collective-permute-start.3 = (bf16[256,256]{1,0:T(8,128)(2,1)S(1)}, bf16[256,256]{1,0:T(8,128)(2,1)S(1)}, u32[]{:S(2)}, u32[]{:S(2)}) collective-permute-start(bf16[256,256]{1,0:T(8,128)(2,1)S(1)} %convolution_convert_fusion), channel_id=1, source_target_pairs={{0,2},{1,3},{2,0},{3,1},{4,6},{5,7},{6,4},{7,5},{8,10},{9,11},{10,... | collective-permute-start | bytes 393224 | tf_op jit(solution)/shard_map/ppermute | solution.py:18
  57.5 68.9 %collective-permute-start.2 = (bf16[256,256]{1,0:T(8,128)(2,1)S(1)}, bf16[256,256]{1,0:T(8,128)(2,1)S(1)}, u32[]{:S(2)}, u32[]{:S(2)}) collective-permute-start(bf16[256,256]{1,0:T(8,128)(2,1)S(1)} %convolution_convert_fusion), channel_id=1, source_target_pairs={{0,1},{1,0},{2,3},{3,2},{4,5},{5,4},{6,7},{7,6},{8,9},{9,8},{10,11... | collective-permute-start | bytes 393224 | tf_op jit(solution)/shard_map/ppermute | solution.py:18
  116.8 9.6 %copy-start.7 = (bf16[256,4096]{1,0:T(8,128)(2,1)}, bf16[256,4096]{1,0:T(8,128)(2,1)S(1)}, u32[]{:S(2)}) copy-start(bf16[256,4096]{1,0:T(8,128)(2,1)S(1)} %collective-permute-done.1.refs_7_) | copy-start | bytes 6291460
  161.6 355.9 %reduce-scatter.5.cloned.1.call-start = ((), (), s32[]{:S(2)}) async-start(), calls=%async_computation.5 | async-start | bytes 28311552 | tf_op jit(solution)/shard_map/reduce_scatter | solution.py:295
  161.7 93.0 %collective-permute-start.6 = (bf16[256,4096]{1,0:T(8,128)(2,1)}, bf16[256,4096]{1,0:T(8,128)(2,1)S(1)}, u32[]{:S(2)}, u32[]{:S(2)}) collective-permute-start(bf16[256,4096]{1,0:T(8,128)(2,1)} %copy-done.11), channel_id=1, source_target_pairs={{0,2},{1,3},{2,0},{3,1},{4,6},{5,7},{6,4},{7,5},{8,10},{9,11},{10,... | collective-permute-start | bytes 6291464 | tf_op jit(solution)/shard_map/ppermute | solution.py:18
  161.7 93.1 %collective-permute-start.5 = (bf16[256,4096]{1,0:T(8,128)(2,1)}, bf16[256,4096]{1,0:T(8,128)(2,1)S(1)}, u32[]{:S(2)}, u32[]{:S(2)}) collective-permute-start(bf16[256,4096]{1,0:T(8,128)(2,1)} %copy-done.11), channel_id=1, source_target_pairs={{0,1},{1,0},{2,3},{3,2},{4,5},{5,4},{6,7},{7,6},{8,9},{9,8},{10,11... | collective-permute-start | bytes 6291464 | tf_op jit(solution)/shard_map/ppermute | solution.py:18
  254.8 1.9 copy-start.9
  256.7 49.8 %copy-start.1 = (bf16[256,8192]{1,0:T(8,128)(2,1)S(1)}, bf16[256,8192]{1,0:T(8,128)(2,1)}, u32[]{:S(2)}) copy-start(bf16[256,8192]{1,0:T(8,128)(2,1)} %tok_ref.1) | copy-start | bytes 12582916
  293.3 7.8 %collective-permute-start.9 = (bf16[256,256]{1,0:T(8,128)(2,1)S(1)}, bf16[256,256]{1,0:T(8,128)(2,1)S(1)}, u32[]{:S(2)}, u32[]{:S(2)}) collective-permute-start(bf16[256,256]{1,0:T(8,128)(2,1)S(1)} %add_convert_fusion.1), channel_id=1, source_target_pairs={{0,3},{1,2},{2,1},{3,0},{4,7},{5,6},{6,5},{7,4},{8,11},{9,10},{10,... | collective-permute-start | bytes 393224 | tf_op jit(solution)/shard_map/ppermute | solution.py:18
  296.0 10.4 %collective-permute-start.8 = (bf16[256,256]{1,0:T(8,128)(2,1)S(1)}, bf16[256,256]{1,0:T(8,128)(2,1)S(1)}, u32[]{:S(2)}, u32[]{:S(2)}) collective-permute-start(bf16[256,256]{1,0:T(8,128)(2,1)S(1)} %add_convert_fusion.1), channel_id=1, source_target_pairs={{0,2},{1,3},{2,0},{3,1},{4,6},{5,7},{6,4},{7,5},{8,10},{9,11},{10,... | collective-permute-start | bytes 393224 | tf_op jit(solution)/shard_map/ppermute | solution.py:18
  296.0 10.4 %collective-permute-start.7 = (bf16[256,256]{1,0:T(8,128)(2,1)S(1)}, bf16[256,256]{1,0:T(8,128)(2,1)S(1)}, u32[]{:S(2)}, u32[]{:S(2)}) collective-permute-start(bf16[256,256]{1,0:T(8,128)(2,1)S(1)} %add_convert_fusion.1), channel_id=1, source_target_pairs={{0,1},{1,0},{2,3},{3,2},{4,5},{5,4},{6,7},{7,6},{8,9},{9,8},{10,11... | collective-permute-start | bytes 393224 | tf_op jit(solution)/shard_map/ppermute | solution.py:18
  328.6 134.6 %collective-permute-start.12 = (bf16[256,4096]{1,0:T(8,128)(2,1)}, bf16[256,4096]{1,0:T(8,128)(2,1)S(1)}, u32[]{:S(2)}, u32[]{:S(2)}) collective-permute-start(bf16[256,4096]{1,0:T(8,128)(2,1)} %copy-done.3), channel_id=1, source_target_pairs={{0,1},{1,0},{2,3},{3,2},{4,5},{5,4},{6,7},{7,6},{8,9},{9,8},{10,11... | collective-permute-start | bytes 6291464 | tf_op jit(solution)/shard_map/ppermute | solution.py:18
  328.7 134.5 %collective-permute-start.13 = (bf16[256,4096]{1,0:T(8,128)(2,1)S(1)}, bf16[256,4096]{1,0:T(8,128)(2,1)S(1)}, u32[]{:S(2)}, u32[]{:S(2)}) collective-permute-start(bf16[256,4096]{1,0:T(8,128)(2,1)S(1)} %get-tuple-element.41), channel_id=1, source_target_pairs={{0,2},{1,3},{2,0},{3,1},{4,6},{5,7},{6,4},{7,5},{8,10},{9,11},{10,... | collective-permute-start | bytes 6291464 | tf_op jit(solution)/shard_map/ppermute | solution.py:18
  331.9 177.8 %collective-permute-start.10 = (bf16[256,4096]{1,0:T(8,128)(2,1)}, bf16[256,4096]{1,0:T(8,128)(2,1)S(1)}, u32[]{:S(2)}, u32[]{:S(2)}) collective-permute-start(bf16[256,4096]{1,0:T(8,128)(2,1)} %copy-done.5), channel_id=1, source_target_pairs={{0,1},{1,0},{2,3},{3,2},{4,5},{5,4},{6,7},{7,6},{8,9},{9,8},{10,11... | collective-permute-start | bytes 6291464 | tf_op jit(solution)/shard_map/ppermute | solution.py:18
  332.0 179.2 %collective-permute-start.11 = (bf16[256,4096]{1,0:T(8,128)(2,1)}, bf16[256,4096]{1,0:T(8,128)(2,1)S(1)}, u32[]{:S(2)}, u32[]{:S(2)}) collective-permute-start(bf16[256,4096]{1,0:T(8,128)(2,1)} %copy-done.4), channel_id=1, source_target_pairs={{0,2},{1,3},{2,0},{3,1},{4,6},{5,7},{6,4},{7,5},{8,10},{9,11},{10,... | collective-permute-start | bytes 6291464 | tf_op jit(solution)/shard_map/ppermute | solution.py:18
  333.6 3.2 copy-start.2
  517.5 3.3 copy-start.6
  (7 other events, 9.5 us)
Sparse Core Ops, SparseCore 0:
  9.9 39.4 all-gather.4
  51.2 36.7 all-gather.2
  161.7 117.1 reduce-scatter.2
  328.7 157.2 reduce-scatter.4

commit v2 on v1

--- a/solution.py
+++ b/solution.py
@@ -32,8 +32,10 @@
 def forward_kernel(n_local, n_remote, has_prev, seq_ref, *refs):
     levels = n_local + n_remote
     sources = refs[:levels]
-    w_ref, up_ref, down_ref, cot_ref = refs[levels : levels + 4]
-    outs = refs[levels + 4 + (2 if has_prev else 0) :]
+    turned = refs[levels : levels + n_local]
+    refs = refs[levels + n_local :]
+    w_ref, up_ref, down_ref, cot_ref = refs[:4]
+    outs = refs[4 + (2 if has_prev else 0) :]
     out_ref, g_ref, wgrad_ref, upsum_ref = outs[:4]
     term_refs = outs[4:]
     hidden = dot(down_ref[...], up_ref[...], 1, 1)
@@ -52,7 +54,11 @@
     for index, term_ref in enumerate(term_refs):
         term_ref[...] = dot(grad, w_ref[0, n_local + index], 1, 1).astype(BF16)
     for level in range(levels):
-        wgrad_ref[0, level] = dot(sources[level][...], grad, 0, 0).astype(BF16)
+        if level < n_local:
+            product = dot(turned[level][...], grad, 1, 0)
+        else:
+            product = dot(sources[level][...], grad, 0, 0)
+        wgrad_ref[0, level] = product.astype(BF16)
 
     @pl.when((pl.program_id(0) == 0) & (pl.program_id(1) == 0))
     def _():
@@ -62,7 +68,7 @@
 
 
 def forward_chunk(
-    chunk, sizes, seq, tokens, remote, weights, up_factor, down_sum, cotangent, prev, extra
+    chunk, sizes, seq, tokens, turned, remote, weights, up_factor, down_sum, cotangent, prev
 ):
     dp, quota, per, n_local, blk = sizes
     rows, features = tokens.shape
@@ -74,6 +80,9 @@
 
     def local_spec(mask):
         return pl.BlockSpec((rows, blk), lambda d, s: (0, block(d, s) ^ mask))
+
+    def turned_spec(mask):
+        return pl.BlockSpec((blk, rows), lambda d, s: (block(d, s) ^ mask, 0))
 
     masks = [0] + [2**bit for bit in range(n_local - 1)]
     packed_spec = pl.BlockSpec((rows, blk), lambda d, s: (0, d * per + s))
@@ -82,6 +91,7 @@
         [pl.BlockSpec(memory_space=pltpu.SMEM)]
         + [local_spec(mask) for mask in masks]
         + [packed_spec for _ in remote]
+        + [turned_spec(mask) for mask in masks]
         + [
             pl.BlockSpec((1, levels, blk, blk), lambda d, s: (block(d, s), 0, 0, 0)),
             pl.BlockSpec((blk, rank), lambda d, s: (block(d, s), 0)),
@@ -90,7 +100,7 @@
         ]
         + [any_spec for _ in prev]
     )
-    args = [seq] + [tokens for _ in masks] + list(remote)
+    args = [seq] + [tokens for _ in masks] + list(remote) + [turned for _ in masks]
     args += [weights, up_factor, down_sum, cotangent] + list(prev)
     aliases = {len(args) - 2: 0, len(args) - 1: 1} if prev else {}
     wide = jax.ShapeDtypeStruct((rows, features), BF16)
@@ -110,7 +120,7 @@
         out_shape=[
             wide,
             wide,
-            jax.ShapeDtypeStruct((dp, per * levels + extra, blk, blk), BF16),
+            jax.ShapeDtypeStruct((dp, per * levels, blk, blk), BF16),
             jax.ShapeDtypeStruct((rows, rank), F32),
         ]
         + [packed for _ in remote],
@@ -125,24 +135,26 @@
     )(*args)
 
 
-def factor_kernel(tok_ref, g_ref, up_ref, down_ref, buf_ref, out_ref):
-    out_ref[0, 0] = dot(tok_ref[...], up_ref[...], 0, 0).astype(BF16)
-    out_ref[0, 1] = dot(g_ref[...], down_ref[...], 0, 0).astype(BF16)
-
-
-def factor_grads(sizes, tokens, grad_hidden, up_sum, down_sum, buffer, offset):
+def factor_kernel(tok_ref, g_ref, up_ref, down_ref, out_ref):
+    blk = out_ref.shape[2]
+    for index in range(out_ref.shape[1] // 2):
+        cols = pl.ds(index * blk, blk)
+        out_ref[0, 2 * index] = dot(tok_ref[:, cols], up_ref[...], 0, 0).astype(BF16)
+        out_ref[0, 2 * index + 1] = dot(g_ref[:, cols], down_ref[...], 0, 0).astype(BF16)
+
+
+def factor_grads(sizes, tokens, grad_hidden, up_sum, down_sum):
     dp, quota, per, n_local, blk = sizes
     rows = tokens.shape[0]
     rank = up_sum.shape[1]
-    col = pl.BlockSpec((rows, blk), lambda d, s: (0, d * quota + s))
-    whole = pl.BlockSpec((rows, rank), lambda d, s: (0, 0))
+    col = pl.BlockSpec((rows, quota * blk), lambda d: (0, d))
+    whole = pl.BlockSpec((rows, rank), lambda d: (0, 0))
     return pl.pallas_call(
         factor_kernel,
-        grid=(dp, quota),
-        in_specs=[col, col, whole, whole, pl.BlockSpec(memory_space=pl.ANY)],
-        out_specs=pl.BlockSpec((1, 2, blk, rank), lambda d, s: (d, offset // 2 + s, 0, 0)),
-        out_shape=jax.ShapeDtypeStruct(buffer.shape, BF16),
-        input_output_aliases={4: 0},
+        grid=(dp,),
+        in_specs=[col, col, whole, whole],
+        out_specs=pl.BlockSpec((1, 2 * quota, blk, rank), lambda d: (d, 0, 0, 0)),
+        out_shape=jax.ShapeDtypeStruct((dp, 2 * quota, blk, rank), BF16),
         compiler_params=pltpu.CompilerParams(vmem_limit_bytes=VMEM_LIMIT),
         cost_estimate=pl.CostEstimate(
             flops=dp * quota * 4 * rows * blk * rank,
@@ -150,7 +162,7 @@
             transcendentals=0,
         ),
         name="factor_grads",
-    )(tokens, grad_hidden, up_sum, down_sum, buffer)
+    )(tokens, grad_hidden, up_sum, down_sum)
 
 
 def backward_kernel(n_local, *refs):
@@ -245,6 +257,7 @@
     down_factor = lax.all_gather(lowrank_down, "dp", axis=0, tiled=True)
     up_factor = lax.all_gather(lowrank_up, "dp", axis=0, tiled=True)
 
+    turned = tokens.T
     arrived = []
     for chunk in range(chunks):
         starts = [(d * chunks + chunk) * width for d in range(dp)]
@@ -260,47 +273,44 @@
     pending, wgrads = [], []
     up_part = None
     for chunk in range(chunks):
-        last = chunk == chunks - 1
         out, grad_hidden, wgrad, up_chunk, *terms = forward_chunk(
             chunk,
             sizes,
             seq_lengths,
             tokens,
+            turned,
             arrived[chunk],
             block_weights,
             up_factor,
             down_sum,
             cotangent,
             prev,
-            2 * quota if last else 0,
         )
         prev = (out, grad_hidden)
         up_part = up_chunk if up_part is None else up_part + up_chunk
         pending.append(terms)
         wgrads.append(wgrad)
-        if not last:
+        if chunk < chunks - 1:
             pending[-1], arrived[chunk + 1] = lax.optimization_barrier((terms, arrived[chunk + 1]))
 
-    scattered = [
-        lax.psum_scatter(wgrad, "dp", scatter_dimension=0, tiled=True) for wgrad in wgrads[:-1]
-    ]
+    scattered = []
+    for wgrad in wgrads:
+        if scattered:
+            wgrad, scattered = lax.optimization_barrier((wgrad, scattered))
+        scattered.append(lax.psum_scatter(wgrad, "dp", scatter_dimension=0, tiled=True))
     up_sum = mp_sum(up_part.astype(BF16))
     returned = [
         [partner(term, "mp", mask) for term, mask in zip(terms, remote_masks)] for terms in pending
     ]
-    merged = factor_grads(
-        sizes, tokens, grad_hidden, up_sum, down_sum, wgrads[-1], per * levels
-    )
-    merged, scattered = lax.optimization_barrier((merged, scattered))
-    scattered.append(lax.psum_scatter(merged, "dp", scatter_dimension=0, tiled=True))
+    factors = factor_grads(sizes, tokens, grad_hidden, up_sum, down_sum)
+    factors = lax.psum_scatter(factors, "dp", scatter_dimension=0, tiled=True)
     partial = backward_local(sizes, grad_hidden, block_weights, up_sum, down_factor)
     grad_tokens = ()
     for chunk in range(chunks):
         grad_tokens = (finish_chunk(chunk, sizes, partial, returned[chunk], grad_tokens),)
 
-    pieces = [part[0, : per * levels] for part in scattered]
-    grad_blocks = jnp.concatenate(pieces, axis=0).reshape(quota, levels, blk, blk)
-    factors = scattered[-1][0, per * levels :].reshape(quota, 2, blk, rank)
+    grad_blocks = jnp.concatenate(scattered, axis=1).reshape(quota, levels, blk, blk)
+    factors = factors.reshape(quota, 2, blk, rank)
     grad_lowrank = jnp.transpose(factors, (0, 2, 1, 3)).reshape(quota * blk, 2, rank)
     return (out, grad_tokens[0], grad_blocks, grad_lowrank)
 

time: 533 us -> 522 us (0.979)
  Pallas kernels: 137 us -> 123 us
    pallas_call x1, Pallas kernels: 22.1 us -> 9.2 us  [factor_grads(): pl.pallas_call(factor_kernel, grid=(dp,), in_specs=[col, col, whole, whol...]
    unnamed x31 -> x30, local copies, waits for them, and re-layouts: 21.4 us -> 25.3 us
  transfers between devices with their start and end apart: 18 -> 19, of which waited for: 12 -> 12; matrix products, arithmetic and copies ran while one was open for 3% -> 5% of each run, Pallas kernels for 19% -> 17%
where the time goes in v2:
time: 522 us; the launch traced here: 521 us
  waiting for transfers between devices  320 us (61%)
  Pallas kernels  123 us (24%)
  local copies, waits for them, and re-layouts  29.5 us (6%)
  starting transfers between devices  23.9 us (5%)
  between operations  14.5 us (3%)
    ppermute x14, waiting for transfers between devices, partner(): return lax.ppermute(value, axis, pairs)  295 us
    pallas_call x2, Pallas kernels, forward_chunk(): pl.pallas_call(functools.partial(forward_kernel, n_local, len(remote), bo...  69.3 us
    pallas_call x1, Pallas kernels, backward_local(): pl.pallas_call(functools.partial(backward_kernel, n_local), grid=(blocks,...  32.2 us
    unnamed x30, local copies, waits for them, and re-layouts  25.3 us
    ppermute x14, starting transfers between devices, partner(): return lax.ppermute(value, axis, pairs)  23.7 us
    all_gather x1, waiting for transfers between devices, per_device(): down_factor = lax.all_gather(lowrank_down, 'dp', axis=0, tiled=True)  23.5 us
    pallas_call x2, Pallas kernels, finish_chunk(): pl.pallas_call(functools.partial(finish_kernel, len(landed)), grid=(dp,),...  12.7 us
  transfers between devices with their start and end apart: 19, of which 12 were waited for; matrix products, arithmetic and copies ran while one was open for 5% of the time, Pallas kernels for 17%

profile of v2, /device:TPU:0, one launch (start us, length us, event | category | flops | bytes accessed | tf_op | source)
XLA Modules:
  0.0 520.6 jit_solution(17304452788841437111)
XLA Ops:
  20.2 4.0 collective-permute-start.1
  25.9 23.5 %all-gather.5.cloned.1.call-done.refs_13_ = bf16[8192,256]{1,0:T(8,128)(2,1)} async-done(((bf16[1024,256]{1,0:T(8,128)(2,1)}), bf16[8192,256]{1,0:T(8,128)(2,1)}) %all-gather.5.cloned.1.call-update) | async-done | bytes 4194320 | tf_op jit(solution)/shard_map/all_gather | solution.py:257
  49.3 4.7 convolution_convert_fusion
  54.1 3.4 collective-permute-start.4
  58.5 6.4 %copy.13 = bf16[256,8192]{0,1:T(8,128)(2,1)} copy(bf16[256,8192]{1,0:T(8,128)(2,1)} %tok_ref.1) | data formatting | bytes 8388608 | tf_op args[0]
  65.5 51.3 %collective-permute-done.1.refs_7_ = bf16[256,4096]{1,0:T(8,128)(2,1)S(1)} collective-permute-done((bf16[256,4096]{1,0:T(8,128)(2,1)}, bf16[256,4096]{1,0:T(8,128)(2,1)S(1)}, u32[]{:S(2)}, u32[]{:S(2)}) %collective-permute-start.1) | collective-permute-done | bytes 2097184 | tf_op jit(solution)/shard_map/ppermute | solution.py:18
  120.2 6.2 %collective-permute-done.3 = bf16[256,256]{1,0:T(8,128)(2,1)S(1)} collective-permute-done((bf16[256,256]{1,0:T(8,128)(2,1)S(1)}, bf16[256,256]{1,0:T(8,128)(2,1)S(1)}, u32[]{:S(2)}, u32[]{:S(2)}) %collective-permute-start.3) | collective-permute-done | bytes 131104 | tf_op jit(solution)/shard_map/ppermute | solution.py:18
  126.5 34.4 %forward_0.1 = (bf16[256,8192]{1,0:T(8,128)(2,1)}, bf16[256,8192]{1,0:T(8,128)(2,1)}, bf16[8,16,256,256]{3,2,1,0:T(8,128)(2,1)}, f32[256,256]{1,0:T(8,128)S(1)},...) custom-call(s32[1]{0:T(128)S(6)} %copy.32.seq_ref, bf16[256,8192]{1,0:T(8,128)(2,1)} %tok_ref.1, ...), custom_call_target="tpu_custom_call" | custom-call | flops 11811160064 | bytes 67108864 | tf_op jit(solution)/shard_map/forward_0/pallas_call | solution.py:109
  162.3 4.1 collective-permute-start.5
  166.4 88.9 %collective-permute-done.6.refs_7_ = bf16[256,4096]{1,0:T(8,128)(2,1)S(1)} collective-permute-done((bf16[256,4096]{1,0:T(8,128)(2,1)}, bf16[256,4096]{1,0:T(8,128)(2,1)S(1)}, u32[]{:S(2)}, u32[]{:S(2)}) %collective-permute-start.6) | collective-permute-done | bytes 2097184 | tf_op jit(solution)/shard_map/ppermute | solution.py:18
  257.2 34.9 %forward_1.1 = (bf16[256,8192]{1,0:T(8,128)(2,1)}, bf16[256,8192]{1,0:T(8,128)(2,1)}, bf16[8,16,256,256]{3,2,1,0:T(8,128)(2,1)}, f32[256,256]{1,0:T(8,128)S(1)},...) custom-call(s32[1]{0:T(128)S(6)} %copy.32.seq_ref, ...), custom_call_target="tpu_custom_call", output_to_operand_aliasing={{0}: (19, {}), {1}: (20, {})} | custom-call | flops 11811160064 | bytes 67108864 | tf_op jit(solution)/shard_map/forward_1/pallas_call | solution.py:109
  294.8 2.5 collective-permute-start.9
  299.3 3.3 collective-permute-done.9
  302.5 5.3 %collective-permute-done.8 = bf16[256,256]{1,0:T(8,128)(2,1)S(1)} collective-permute-done((bf16[256,256]{1,0:T(8,128)(2,1)S(1)}, bf16[256,256]{1,0:T(8,128)(2,1)S(1)}, u32[]{:S(2)}, u32[]{:S(2)}) %collective-permute-start.8) | collective-permute-done | bytes 131104 | tf_op jit(solution)/shard_map/ppermute | solution.py:18
  307.9 9.2 %factor_grads.1 = bf16[8,8,256,256]{3,2,1,0:T(8,128)(2,1)} custom-call(bf16[256,8192]{1,0:T(8,128)(2,1)S(1)} %copy-done.1, bf16[256,8192]{1,0:T(8,128)(2,1)} %get-tuple-element.35.refs_0_.refs_1_.refs_2_.refs_3_.refs_4_.refs_5_.g_ref, bf16[256,256]{1,0:T(8,128)(2,1)S(1)} %add_convert_fusion.refs_12_.up_ref, ...), custom_call_target="tpu_custom_call" | custom-call | flops 2147483648 | bytes 16777216 | tf_op jit(solution)/shard_map/factor_grads/pallas_call | solution.py:152
  317.8 3.2 collective-permute-start.13
  322.8 2.3 copy-done.2
  325.1 32.2 %backward_local.1.refs_0_ = f32[256,8192]{1,0:T(8,128)} custom-call(bf16[256,8192]{1,0:T(8,128)(2,1)S(1)} %copy-done.2, bf16[256,8192]{1,0:T(8,128)(2,1)S(1)} %copy-done.2, bf16[256,8192]{1,0:T(8,128)(2,1)S(1)} %copy-done.2, bf16[256,8192]{1,0:T(8,128)(2,1)S(1)} %copy-done.2, bf16[256,8192]{1,0:T(8,128)(2,1)S(1)} %copy-done.2, ...), custom_call_target="tpu_custom_call" | custom-call | flops 7516192768 | bytes 67108864 | tf_op jit(solution)/shard_map/backward_local/pallas_call | solution.py:190
  357.3 95.1 %collective-permute-done.12.refs_1_ = bf16[256,4096]{1,0:T(8,128)(2,1)S(1)} collective-permute-done((bf16[256,4096]{1,0:T(8,128)(2,1)}, bf16[256,4096]{1,0:T(8,128)(2,1)S(1)}, u32[]{:S(2)}, u32[]{:S(2)}) %collective-permute-start.12) | collective-permute-done | bytes 2097184 | tf_op jit(solution)/shard_map/ppermute | solution.py:18
  452.4 6.4 %finish_0.1.refs_3_ = bf16[256,8192]{1,0:T(8,128)(2,1)} custom-call(f32[256,8192]{1,0:T(8,128)} %backward_local.1.refs_0_, bf16[256,4096]{1,0:T(8,128)(2,1)S(1)} %collective-permute-done.12.refs_1_, bf16[256,4096]{1,0:T(8,128)(2,1)S(1)} %collective-permute-done.13.refs_2_), custom_call_target="tpu_custom_call" | custom-call | flops 3145728 | bytes 10485760 | tf_op jit(solution)/shard_map/finish_0/pallas_call | solution.py:225
  458.8 40.1 %collective-permute-done.10.refs_1_ = bf16[256,4096]{1,0:T(8,128)(2,1)S(1)} collective-permute-done((bf16[256,4096]{1,0:T(8,128)(2,1)}, bf16[256,4096]{1,0:T(8,128)(2,1)S(1)}, u32[]{:S(2)}, u32[]{:S(2)}) %collective-permute-start.10) | collective-permute-done | bytes 2097184 | tf_op jit(solution)/shard_map/ppermute | solution.py:18
  500.3 6.3 %finish_1.1 = bf16[256,8192]{1,0:T(8,128)(2,1)} custom-call(f32[256,8192]{1,0:T(8,128)} %backward_local.1.refs_0_, bf16[256,4096]{1,0:T(8,128)(2,1)S(1)} %collective-permute-done.10.refs_1_, bf16[256,4096]{1,0:T(8,128)(2,1)S(1)} %collective-permute-done.11.refs_2_, bf16[256,8192]{1,0:T(8,128)(2,1)} %finish_0.1.refs_3_), custom_call_target="tpu_custom_call", output_to_operand_aliasing={{}: (3, {})} | custom-call | flops 3145728 | bytes 10485760 | tf_op jit(solution)/shard_map/finish_1/pallas_call | solution.py:225
  506.7 3.4 copy.14
  510.1 4.0 pad_maximum_fusion
  (62 shorter events, 31.1 us)
Async XLA Ops:
  7.2 42.2 %all-gather.5.cloned.1.call-start = ((), (), s32[]{:S(2)}) async-start(), calls=%async_computation.4 | async-start | bytes 4718592 | tf_op jit(solution)/shard_map/all_gather | solution.py:257
  7.9 118.5 %all-gather.3.cloned.1.call-start = ((), (), s32[]{:S(2)}) async-start(), calls=%async_computation.3 | async-start | bytes 4718592 | tf_op jit(solution)/shard_map/all_gather | solution.py:258
  8.6 308.6 %reduce-scatter.4.cloned.1.call-start = ((), (), s32[]{:S(2)}) async-start(), calls=%async_computation.5 | async-start | bytes 18874368 | tf_op jit(solution)/shard_map/reduce_scatter | solution.py:300
  8.7 7.2 %copy-start = (bf16[256,8192]{1,0:T(8,128)(2,1)S(1)}, bf16[256,8192]{1,0:T(8,128)(2,1)}, u32[]{:S(2)}) copy-start(bf16[256,8192]{1,0:T(8,128)(2,1)} %tok_ref.1) | copy-start | bytes 12582916
  20.2 96.6 %collective-permute-start.1 = (bf16[256,4096]{1,0:T(8,128)(2,1)}, bf16[256,4096]{1,0:T(8,128)(2,1)S(1)}, u32[]{:S(2)}, u32[]{:S(2)}) collective-permute-start(bf16[256,4096]{1,0:T(8,128)(2,1)} %get-tuple-element.46), channel_id=1, source_target_pairs={{0,2},{1,3},{2,0},{3,1},{4,6},{5,7},{6,4},{7,5},{8,10},{9,11},{10,... | collective-permute-start | bytes 6291464 | tf_op jit(solution)/shard_map/ppermute | solution.py:18
  24.3 94.8 %collective-permute-start = (bf16[256,4096]{1,0:T(8,128)(2,1)}, bf16[256,4096]{1,0:T(8,128)(2,1)}, u32[]{:S(2)}, u32[]{:S(2)}) collective-permute-start(bf16[256,4096]{1,0:T(8,128)(2,1)} %get-tuple-element.46), channel_id=1, source_target_pairs={{0,1},{1,0},{2,3},{3,2},{4,5},{5,4},{6,7},{7,6},{8,9},{9,8},{10,11... | collective-permute-start | bytes 6291464 | tf_op jit(solution)/shard_map/ppermute | solution.py:18
  54.1 66.1 %collective-permute-start.4 = (bf16[256,256]{1,0:T(8,128)(2,1)S(1)}, bf16[256,256]{1,0:T(8,128)(2,1)S(1)}, u32[]{:S(2)}, u32[]{:S(2)}) collective-permute-start(bf16[256,256]{1,0:T(8,128)(2,1)S(1)} %convolution_convert_fusion), channel_id=1, source_target_pairs={{0,3},{1,2},{2,1},{3,0},{4,7},{5,6},{6,5},{7,4},{8,11},{9,10},{10,... | collective-permute-start | bytes 393224 | tf_op jit(solution)/shard_map/ppermute | solution.py:18
  57.4 68.9 %collective-permute-start.3 = (bf16[256,256]{1,0:T(8,128)(2,1)S(1)}, bf16[256,256]{1,0:T(8,128)(2,1)S(1)}, u32[]{:S(2)}, u32[]{:S(2)}) collective-permute-start(bf16[256,256]{1,0:T(8,128)(2,1)S(1)} %convolution_convert_fusion), channel_id=1, source_target_pairs={{0,2},{1,3},{2,0},{3,1},{4,6},{5,7},{6,4},{7,5},{8,10},{9,11},{10,... | collective-permute-start | bytes 393224 | tf_op jit(solution)/shard_map/ppermute | solution.py:18
  57.5 68.9 %collective-permute-start.2 = (bf16[256,256]{1,0:T(8,128)(2,1)S(1)}, bf16[256,256]{1,0:T(8,128)(2,1)S(1)}, u32[]{:S(2)}, u32[]{:S(2)}) collective-permute-start(bf16[256,256]{1,0:T(8,128)(2,1)S(1)} %convolution_convert_fusion), channel_id=1, source_target_pairs={{0,1},{1,0},{2,3},{3,2},{4,5},{5,4},{6,7},{7,6},{8,9},{9,8},{10,11... | collective-permute-start | bytes 393224 | tf_op jit(solution)/shard_map/ppermute | solution.py:18
  116.8 9.7 %copy-start.6 = (bf16[256,4096]{1,0:T(8,128)(2,1)}, bf16[256,4096]{1,0:T(8,128)(2,1)S(1)}, u32[]{:S(2)}) copy-start(bf16[256,4096]{1,0:T(8,128)(2,1)S(1)} %collective-permute-done.1.refs_7_) | copy-start | bytes 6291460
  162.2 344.5 %reduce-scatter.8.cloned.1.call-start = ((), (), s32[]{:S(2)}) async-start(), calls=%async_computation.7 | async-start | bytes 9437184 | tf_op jit(solution)/shard_map/reduce_scatter | solution.py:306
  162.2 93.0 %collective-permute-start.6 = (bf16[256,4096]{1,0:T(8,128)(2,1)}, bf16[256,4096]{1,0:T(8,128)(2,1)S(1)}, u32[]{:S(2)}, u32[]{:S(2)}) collective-permute-start(bf16[256,4096]{1,0:T(8,128)(2,1)} %copy-done.10), channel_id=1, source_target_pairs={{0,2},{1,3},{2,0},{3,1},{4,6},{5,7},{6,4},{7,5},{8,10},{9,11},{10,... | collective-permute-start | bytes 6291464 | tf_op jit(solution)/shard_map/ppermute | solution.py:18
  162.3 93.1 %collective-permute-start.5 = (bf16[256,4096]{1,0:T(8,128)(2,1)}, bf16[256,4096]{1,0:T(8,128)(2,1)S(1)}, u32[]{:S(2)}, u32[]{:S(2)}) collective-permute-start(bf16[256,4096]{1,0:T(8,128)(2,1)} %copy-done.10), channel_id=1, source_target_pairs={{0,1},{1,0},{2,3},{3,2},{4,5},{5,4},{6,7},{7,6},{8,9},{9,8},{10,11... | collective-permute-start | bytes 6291464 | tf_op jit(solution)/shard_map/ppermute | solution.py:18
  257.2 50.7 %copy-start.1 = (bf16[256,8192]{1,0:T(8,128)(2,1)S(1)}, bf16[256,8192]{1,0:T(8,128)(2,1)}, u32[]{:S(2)}) copy-start(bf16[256,8192]{1,0:T(8,128)(2,1)} %tok_ref.1) | copy-start | bytes 12582916
  294.8 7.7 %collective-permute-start.9 = (bf16[256,256]{1,0:T(8,128)(2,1)S(1)}, bf16[256,256]{1,0:T(8,128)(2,1)S(1)}, u32[]{:S(2)}, u32[]{:S(2)}) collective-permute-start(bf16[256,256]{1,0:T(8,128)(2,1)S(1)} %add_convert_fusion.1), channel_id=1, source_target_pairs={{0,3},{1,2},{2,1},{3,0},{4,7},{5,6},{6,5},{7,4},{8,11},{9,10},{10,... | collective-permute-start | bytes 393224 | tf_op jit(solution)/shard_map/ppermute | solution.py:18
  297.4 10.5 %collective-permute-start.8 = (bf16[256,256]{1,0:T(8,128)(2,1)S(1)}, bf16[256,256]{1,0:T(8,128)(2,1)S(1)}, u32[]{:S(2)}, u32[]{:S(2)}) collective-permute-start(bf16[256,256]{1,0:T(8,128)(2,1)S(1)} %add_convert_fusion.1), channel_id=1, source_target_pairs={{0,2},{1,3},{2,0},{3,1},{4,6},{5,7},{6,4},{7,5},{8,10},{9,11},{10,... | collective-permute-start | bytes 393224 | tf_op jit(solution)/shard_map/ppermute | solution.py:18
  297.4 10.5 %collective-permute-start.7 = (bf16[256,256]{1,0:T(8,128)(2,1)S(1)}, bf16[256,256]{1,0:T(8,128)(2,1)S(1)}, u32[]{:S(2)}, u32[]{:S(2)}) collective-permute-start(bf16[256,256]{1,0:T(8,128)(2,1)S(1)} %add_convert_fusion.1), channel_id=1, source_target_pairs={{0,1},{1,0},{2,3},{3,2},{4,5},{5,4},{6,7},{7,6},{8,9},{9,8},{10,11... | collective-permute-start | bytes 393224 | tf_op jit(solution)/shard_map/ppermute | solution.py:18
  317.2 192.9 %reduce-scatter.6.cloned.1.call-start = ((), (), s32[]{:S(2)}) async-start(), calls=%async_computation.6 | async-start | bytes 18874368 | tf_op jit(solution)/shard_map/reduce_scatter | solution.py:300
  317.7 134.6 %collective-permute-start.12 = (bf16[256,4096]{1,0:T(8,128)(2,1)}, bf16[256,4096]{1,0:T(8,128)(2,1)S(1)}, u32[]{:S(2)}, u32[]{:S(2)}) collective-permute-start(bf16[256,4096]{1,0:T(8,128)(2,1)} %copy-done.3), channel_id=1, source_target_pairs={{0,1},{1,0},{2,3},{3,2},{4,5},{5,4},{6,7},{7,6},{8,9},{9,8},{10,11... | collective-permute-start | bytes 6291464 | tf_op jit(solution)/shard_map/ppermute | solution.py:18
  317.8 134.6 %collective-permute-start.13 = (bf16[256,4096]{1,0:T(8,128)(2,1)S(1)}, bf16[256,4096]{1,0:T(8,128)(2,1)S(1)}, u32[]{:S(2)}, u32[]{:S(2)}) collective-permute-start(bf16[256,4096]{1,0:T(8,128)(2,1)S(1)} %get-tuple-element.41), channel_id=1, source_target_pairs={{0,2},{1,3},{2,0},{3,1},{4,6},{5,7},{6,4},{7,5},{8,10},{9,11},{10,... | collective-permute-start | bytes 6291464 | tf_op jit(solution)/shard_map/ppermute | solution.py:18
  321.0 177.9 %collective-permute-start.10 = (bf16[256,4096]{1,0:T(8,128)(2,1)}, bf16[256,4096]{1,0:T(8,128)(2,1)S(1)}, u32[]{:S(2)}, u32[]{:S(2)}) collective-permute-start(bf16[256,4096]{1,0:T(8,128)(2,1)} %copy-done.5), channel_id=1, source_target_pairs={{0,1},{1,0},{2,3},{3,2},{4,5},{5,4},{6,7},{7,6},{8,9},{9,8},{10,11... | collective-permute-start | bytes 6291464 | tf_op jit(solution)/shard_map/ppermute | solution.py:18
  321.1 179.2 %collective-permute-start.11 = (bf16[256,4096]{1,0:T(8,128)(2,1)}, bf16[256,4096]{1,0:T(8,128)(2,1)S(1)}, u32[]{:S(2)}, u32[]{:S(2)}) collective-permute-start(bf16[256,4096]{1,0:T(8,128)(2,1)} %copy-done.4), channel_id=1, source_target_pairs={{0,2},{1,3},{2,0},{3,1},{4,6},{5,7},{6,4},{7,5},{8,10},{9,11},{10,... | collective-permute-start | bytes 6291464 | tf_op jit(solution)/shard_map/ppermute | solution.py:18
  322.8 2.3 copy-start.2
  506.6 3.4 copy-start.9
  (6 other events, 8.6 us)
Sparse Core Ops, SparseCore 0:
  9.9 39.4 all-gather.4
  51.2 36.7 all-gather.2
  162.3 117.1 reduce-scatter.3
  317.3 71.6 reduce-scatter.7
  392.8 115.9 reduce-scatter.5
